TPU v7x, 256 devices: a whole 4x4x8 slice. The times are simulated.
256 devices in a mesh: fsdp: 32 (over z, x_lo, core), tenant: 4 (over y), tensor: 2 (over x_hi).
Axes of the slice: x: 4 (x_hi: 2, x_lo: 2; x = x_hi * 2 + x_lo), y: 4, z: 8, core: 2. Of those that a mesh axis runs over, the one named last changes fastest.
Arguments:
- tokens: bfloat16 [16384, 8192], P(('fsdp', 'tenant')), may hold values from -6 to 6
- inner_x: bfloat16 [16384, 8192], P(('fsdp', 'tenant'), 'tensor'), may hold values from -6 to 6
- step_size: float32 [16384, 128], P(('fsdp', 'tenant'), 'tensor'), may hold values from 0.01 to 0.25
- decay_rate: float32 [128], P('tensor'), may hold values from 0.2 to 16
- grad_out: bfloat16 [16384, 8192], P(('fsdp', 'tenant'), 'tensor'), may hold values from -6 to 6
- w_bc: bfloat16 [8192, 2048], P('fsdp', 'tensor'), may hold values from -0.0625 to 0.0625
- a_store: bfloat16 [256, 8192, 64], P(('fsdp', 'tenant'), 'tensor'), may hold values from -0.0625 to 0.0625
- b_store: bfloat16 [256, 64, 2048], P(('fsdp', 'tenant'), None, 'tensor'), may hold values from -0.75 to 0.75
- tenant_list: int32 [4, 2], P('tenant'), may hold values from 0 to 255, as said below
- block_slot: int32 [128], P(('fsdp', 'tenant')), may hold values from 0 to 1, as said below
- owner_slot: int32 [256], replicated, may hold values from 0 to 255, as said below
Outputs:
- mixed_out: bfloat16 [16384, 8192], P(('fsdp', 'tenant'), 'tensor')
- input_grad: bfloat16 [16384, 8192], P(('fsdp', 'tenant'), 'tensor')
- a_grad: bfloat16 [256, 8192, 64], P(('fsdp', 'tenant'), 'tensor')
- b_grad: bfloat16 [256, 64, 2048], P(('fsdp', 'tenant'), None, 'tensor')
Inputs may be any that keep to these rules, and one draw needn't show every extreme that they name: `tenant_list`: row g lists the tenants of data group g; entries of a row are distinct. `block_slot`: sample b belongs to data group (b) mod 4. In each group the positions used are 0 up to some count, each used by some sample; the count is 2 in some group. Tenant t's adapters are row owner_slot[t] of a_store and b_store; every row belongs to exactly one tenant. The row owner_slot[tenant_list[g, j]] lies on the devices of tenant index (g + 2 - j) mod 4.
All inputs are finite; a program needn't handle non-finite values.
Results may differ from a plain program's by a relative error of at most 0.012.
Values may be sent and summed in bfloat16 or wider, within the bound.
A program may use at most 320 MiB of HBM per device.

v0:
```python
import jax
import jax.numpy as jnp
from jax import lax
from jax.sharding import PartitionSpec as P

HEADS_GRP = 32
NS = 256


def spread_2(block, axis, holder):
    block = jnp.where(lax.axis_index(axis) == holder, block, jnp.zeros_like(block))
    return lax.psum(block, axis)


def mix_state(proj_in, inner_x, step_size, decay_rate, block_len, heads_grp, state_dim):
    length = proj_in.shape[0]
    nblock = length // block_len
    groups = proj_in.shape[1] // (2 * state_dim)
    num_heads = decay_rate.shape[0]
    head_dim = inner_x.shape[1] // num_heads
    split_proj = proj_in.reshape(nblock, block_len, groups, 2, state_dim)
    b_input = split_proj[:, :, :, 0, :]
    c_output = split_proj[:, :, :, 1, :]
    values = inner_x.astype(jnp.float32).reshape(nblock, block_len, groups, heads_grp, head_dim)
    step_blk = step_size.reshape(nblock, block_len, groups, heads_grp)
    log_decay = -step_blk * decay_rate.reshape(groups, heads_grp)
    totals = jnp.cumsum(log_decay, axis=1)
    spread = totals[:, :, None] - totals[:, None, :]
    causal = jnp.arange(block_len)[:, None] >= jnp.arange(block_len)[None, :]
    decay_mat = jnp.exp(jnp.where(causal[None, :, :, None, None], spread, -1e30))
    scores = jnp.einsum("ntgk,nsgk->ntsg", c_output, b_input, precision=lax.Precision.HIGHEST)
    weight = decay_mat * scores[..., None] * step_blk[:, None]
    mixed_all = jnp.einsum("ntsgh,nsghp->ntghp", weight, values, precision=lax.Precision.HIGHEST)
    return mixed_all.reshape(length, num_heads * head_dim)


def shards(
    tokens,
    inner_x,
    step_size,
    decay_rate,
    grad_out,
    w_bc,
    a_store,
    b_store,
    tenant_list,
    block_slot,
    owner_slot,
):
    tenant_span = lax.axis_size("tenant")
    fsdp_here = lax.axis_index("fsdp")
    tensor_here = lax.axis_index("tensor")
    owned = a_store.shape[0]
    width_half = a_store.shape[1]
    length = tokens.shape[0]
    nblock = block_slot.shape[0]
    block_len = length // nblock
    list_len = tenant_list.shape[1]
    columns = w_bc.shape[1]
    my_list = tenant_list[0]
    location = owner_slot[my_list]
    holder = location // owned
    root_fsdp = holder // tenant_span
    pool_index = holder % tenant_span * owned + location % owned
    pool_a, pool_b = (
        lax.all_gather(a_store, "tenant", axis=0, tiled=True),
        lax.all_gather(b_store, "tenant", axis=0, tiled=True),
    )
    fetched_a = []
    fetched_b = []
    for position in range(list_len):
        got_a, got_b = (
            spread_2(pool_a[pool_index[position]], "fsdp", root_fsdp[position]),
            spread_2(pool_b[pool_index[position]], "fsdp", root_fsdp[position]),
        )
        fetched_a.append(got_a)
        fetched_b.append(got_b)
    list_a = jnp.stack(fetched_a)
    list_b = jnp.stack(fetched_b)
    token_half = lax.dynamic_slice_in_dim(tokens, tensor_here * width_half, width_half, 1)
    sel_a = list_a[block_slot]
    sel_b = list_b[block_slot]
    half_blocks = token_half.reshape(nblock, block_len, width_half)
    part_low = jnp.einsum("nbd,ndr->nbr", half_blocks, sel_a, preferred_element_type=jnp.float32)
    low_rank = lax.psum(part_low, "tensor").astype(jnp.bfloat16)
    whole_w = lax.all_gather(w_bc, "fsdp", axis=0, tiled=True)
    base_proj = jnp.dot(tokens, whole_w, preferred_element_type=jnp.float32)
    adapter_proj = jnp.einsum("nbr,nrc->nbc", low_rank, sel_b, preferred_element_type=jnp.float32)
    proj = (base_proj + adapter_proj.reshape(length, columns)).astype(jnp.bfloat16)

    def mixer(proj_in):
        return mix_state(proj_in, inner_x, step_size, decay_rate, block_len, HEADS_GRP, NS)

    mixed_now, pull_back = jax.vjp(mixer, proj.astype(jnp.float32))
    (grad_proj,) = pull_back(grad_out.astype(jnp.float32))
    grad_proj = grad_proj.astype(jnp.bfloat16)
    grad_blocks = grad_proj.reshape(nblock, block_len, columns)
    part_q = jnp.einsum("nbc,nrc->nbr", grad_blocks, sel_b, preferred_element_type=jnp.float32)
    q_low = lax.psum(part_q, "tensor").astype(jnp.bfloat16)
    part_input = jnp.dot(grad_proj, whole_w.T, preferred_element_type=jnp.float32)
    summed_input = lax.psum_scatter(part_input, "tensor", scatter_dimension=1, tiled=True)
    adapter_input = jnp.einsum("nbr,ndr->nbd", q_low, sel_a, preferred_element_type=jnp.float32)
    input_grad = (summed_input + adapter_input.reshape(length, width_half)).astype(jnp.bfloat16)
    grad_a_blk = jnp.einsum("nbd,nbr->ndr", half_blocks, q_low, preferred_element_type=jnp.float32)
    grad_b_blk = jnp.einsum(
        "nbr,nbc->ncr", low_rank, grad_blocks, preferred_element_type=jnp.float32
    )
    chosen = (block_slot[:, None] == jnp.arange(list_len)[None, :]).astype(jnp.float32)
    list_grad_a = jnp.einsum("nl,ndr->ldr", chosen, grad_a_blk, precision=lax.Precision.HIGHEST)
    list_grad_b = jnp.einsum("nl,ncr->lcr", chosen, grad_b_blk, precision=lax.Precision.HIGHEST)
    group_a, group_b = lax.psum((list_grad_a, list_grad_b), "fsdp")
    round_a = group_a.astype(jnp.bfloat16)
    round_b = group_b.astype(jnp.bfloat16)
    round_b = jnp.swapaxes(round_b, 1, 2)
    send_hot = (
        (pool_index[:, None] == jnp.arange(tenant_span * owned)[None, :])
        & (root_fsdp == fsdp_here)[:, None]
    ).astype(jnp.bfloat16)
    send_a = jnp.einsum("lk,ldr->kdr", send_hot, round_a, preferred_element_type=jnp.float32)
    send_b = jnp.einsum("lk,lrc->krc", send_hot, round_b, preferred_element_type=jnp.float32)
    owner_a, owner_b = (
        lax.psum_scatter(
            send_a.astype(jnp.bfloat16), "tenant", scatter_dimension=0, tiled=True
        ).astype(jnp.float32),
        lax.psum_scatter(
            send_b.astype(jnp.bfloat16), "tenant", scatter_dimension=0, tiled=True
        ).astype(jnp.float32),
    )
    return (
        mixed_now.astype(jnp.bfloat16),
        input_grad,
        owner_a.astype(jnp.bfloat16),
        owner_b.astype(jnp.bfloat16),
    )


def solution(mesh):
    placed = (
        P(("fsdp", "tenant"), None),
        P(("fsdp", "tenant"), "tensor"),
        P(("fsdp", "tenant"), "tensor"),
        P("tensor"),
        P(("fsdp", "tenant"), "tensor"),
        P("fsdp", "tensor"),
        P(("fsdp", "tenant"), "tensor", None),
        P(("fsdp", "tenant"), None, "tensor"),
        P("tenant", None),
        P(("fsdp", "tenant")),
        P(),
    )
    return jax.shard_map(
        shards,
        mesh=mesh,
        in_specs=placed,
        out_specs=(
            P(("fsdp", "tenant"), "tensor"),
            P(("fsdp", "tenant"), "tensor"),
            P(("fsdp", "tenant"), "tensor", None),
            P(("fsdp", "tenant"), None, "tensor"),
        ),
        check_vma=False,
    )
```

profile of v0, /device:TPU:1, one launch (start us, length us, event | category | flops | bytes accessed | tf_op | source)
XLA Modules:
  0.0 696.6 jit_solution(18225526234914856644)
XLA Ops:
  7.3 0.7 all-gather.8.cloned.1.call-update
  8.0 0.7 all-gather.6.cloned.1.call-update
  8.7 0.7 fusion.52
  9.4 1.3 gather_fusion
  11.3 0.6 fusion.62
  17.7 21.7 %all-gather.8.cloned.1.call-done = bf16[8,64,1024]{2,1,0:T(8,128)(2,1)} async-done(((bf16[2,64,1024]{2,1,0:T(8,128)(2,1)}), bf16[8,64,1024]{2,1,0:T(8,128)(2,1)}) %all-gather.8.cloned.1.call-update) | async-done | bytes 1048592 | tf_op jit(solution)/shard_map/all_gather | solution.py:67
  39.3 1.7 dynamic-slice_select_fusion.2
  41.0 52.2 %all-gather.6.cloned.1.call-done = bf16[8,4096,64]{1,2,0:T(8,128)(2,1)} async-done(((bf16[2,4096,64]{1,2,0:T(8,128)(2,1)}), bf16[8,4096,64]{1,2,0:T(8,128)(2,1)}) %all-gather.6.cloned.1.call-update) | async-done | bytes 4194320 | tf_op jit(solution)/shard_map/all_gather | solution.py:66
  93.3 2.2 dynamic-slice_select_fusion
  97.2 1.3 copy.51
  98.5 1.6 copy.54
  100.2 3.6 fusion.2
  103.8 222.9 %all-reduce.7.cloned.1.call-done = (bf16[1,4096,64]{1,2,0:T(8,128)(2,1)}, bf16[1,4096,64]{1,2,0:T(8,128)(2,1)}, bf16[1,64,1024]{2,1,0:T(8,128)(2,1)}, bf16[1,64,1024]{2,1,0:T(8,128)(2,1)}) async-done(((bf16[1,4096,64]{1,2,0:T(8,128)(2,1)}, bf16[1,4096,64]{1,2,0:T(8,128)(2,1)}, bf16[1,64,1024]{2,1,0:T(8,128)(2,1)}, bf16[1,64,1024]{2,1,0:T(8,128)(2,1)}), (bf16[1,4096,64]{1,2,0:T(8,128)(2,1)}, ...) | async-done | bytes 1310736 | tf_op jit(solution)/shard_map/psum | solution.py:12
  326.7 1.5 convolution_bitcast_fusion.3
  328.2 8.9 %psum.58 = bf16[1,128,64]{1,2,0:T(8,128)(2,1)S(1)} all-reduce(f32[1,128,64]{1,2,0:T(8,128)S(1)} %convolution_bitcast_fusion.3), channel_id=1, replica_groups=mesh['fsdp'=32,'tenant'=4,'tensor'=2] {'tensor'}, use_global_device_ids=true, to_apply=%region_3.4 | all-reduce | flops 8192 | bytes 49152 | tf_op jit(solution)/shard_map/psum | solution.py:85
  337.2 91.7 %all-gather.4.cloned.1.call-done = bf16[8192,1024]{1,0:T(8,128)(2,1)} async-done(((bf16[256,1024]{1,0:T(8,128)(2,1)}), bf16[8192,1024]{1,0:T(8,128)(2,1)}) %all-gather.4.cloned.1.call-update) | async-done | bytes 16777232 | tf_op jit(solution)/shard_map/all_gather | solution.py:86
  428.8 8.1 %fusion.63 = f32[128,1024]{1,0:T(8,128)S(1)} fusion(bf16[128,8192]{1,0:T(8,128)(2,1)S(1)} %copy-done, bf16[8192,1024]{1,0:T(8,128)(2,1)} %all-gather.4.cloned.1.call-done), kind=kOutput, calls=%fused_computation.97 | convolution fusion | flops 2147483648 | bytes 19398656 | tf_op jit(solution)/shard_map/dot_general | solution.py:87
  439.0 13.5 %fusion.64 = f32[128,8192]{1,0:T(8,128)} fusion(bf16[128,1024]{0,1:T(8,128)(2,1)S(1)} %bitcast.109, bf16[8192,1024]{1,0:T(8,128)(2,1)} %all-gather.4.cloned.1.call-done), kind=kOutput, calls=%fused_computation.98 | convolution fusion | flops 2147483648 | bytes 21233664 | tf_op jit(solution)/shard_map/dot_general | solution.py:100
  453.0 1.1 convolution_bitcast_fusion.4
  454.1 9.6 %psum.61 = bf16[1,128,64]{1,2,0:T(8,128)(2,1)S(1)} all-reduce(f32[1,128,64]{1,2,0:T(8,128)S(1)} %convolution_bitcast_fusion.4), channel_id=1, replica_groups=mesh['fsdp'=32,'tenant'=4,'tensor'=2] {'tensor'}, use_global_device_ids=true, to_apply=%region_8.9 | all-reduce | flops 8192 | bytes 49152 | tf_op jit(solution)/shard_map/psum | solution.py:99
  464.1 3.2 broadcast_multiply_fusion
  467.3 137.3 %all-reduce.8 = (bf16[2,4096,64]{1,0,2:T(2,128)(2,1)}, bf16[2,1024,64]{1,0,2:T(2,128)(2,1)}) all-reduce(f32[2,4096,64]{1,0,2:T(2,128)} %broadcast_multiply_fusion, f32[2,1024,64]{1,0,2:T(2,128)S(1)} %broadcast_multiply_fusion.1), channel_id=1, replica_groups=mesh['fsdp'=32,'tenant'=4,'tensor'=2] {'fsdp'}, use_global_device_ids=true, to_apply=%region_9.10 | all-reduce | flops 655360 | bytes 3932160 | tf_op jit(solution)/shard_map/psum | solution.py:111
  604.6 1.6 convolution_convert_fusion.1
  606.2 1.6 copy.58
  607.8 1.9 convolution_convert_fusion
  609.7 4.2 copy.57
  614.0 1.2 convolution_bitcast_fusion.2
  615.3 7.0 %fusion.15 = bf16[2,32,128,64]{2,3,1,0:T(8,128)(2,1)} fusion(bf16[128,2,32,64]{0,3,2,1:T(8,128)(2,1)S(1)} %bitcast.113, f32[128,2,32]{0,2,1:T(8,128)} %bitcast.116, f32[128,128,2]{1,0,2:T(8,128)S(1)} %copy.50, f32[128,2,32]{0,2,1:T(8,128)} %copy-done.9, pred[128,128]{1,0:T(8,128)(4,1)} %copy-done.10), kind=kOutput, calls=%fused_computation.19 | convolution fusion | flops 810024960 | bytes 2310144 | tf_op jit(solution)/shard_map/jvp(ntsgh,nsghp->ntghp)/dot_general | solution.py:33
  622.3 2.3 copy.59
  624.6 3.2 fusion
  627.8 8.2 %reduce-scatter.8.cloned.1.call-done = bf16[2,64,1024]{2,1,0:T(8,128)(2,1)} async-done(((bf16[8,64,1024]{2,1,0:T(8,128)(2,1)}), bf16[2,64,1024]{2,1,0:T(8,128)(2,1)}) %reduce-scatter.8.cloned.1.call-update) | async-done | bytes 262160 | tf_op jit(solution)/shard_map/reduce_scatter | solution.py:125
  636.0 53.8 %reduce-scatter.6.cloned.1.call-done = bf16[2,4096,64]{1,2,0:T(8,128)(2,1)} async-done(((bf16[8,4096,64]{1,2,0:T(8,128)(2,1)}), bf16[2,4096,64]{1,2,0:T(8,128)(2,1)}) %reduce-scatter.6.cloned.1.call-update) | async-done | bytes 1048592 | tf_op jit(solution)/shard_map/reduce_scatter | solution.py:122
  (66 shorter events, 5.3 us)
Async XLA Ops:
  7.2 319.5 %copy-start = (bf16[128,8192]{1,0:T(8,128)(2,1)S(1)}, bf16[128,8192]{1,0:T(8,128)(2,1)}, u32[]{:S(2)}) copy-start(bf16[128,8192]{1,0:T(8,128)(2,1)} %param.11) | copy-start | bytes 6291460
  7.2 89.6 %copy-start.15 = (f32[64]{0:T(128)S(1)}, f32[64]{0:T(128)}, u32[]{:S(2)}) copy-start(f32[64]{0:T(128)} %param.14) | copy-start | bytes 772
  7.2 89.7 %copy-start.8 = (f32[128,64]{0,1:T(8,128)S(1)}, f32[128,64]{0,1:T(8,128)}, u32[]{:S(2)}) copy-start(f32[128,64]{0,1:T(8,128)} %param.13) | copy-start | bytes 98308
  7.2 90.0 %copy-start.1 = (bf16[128,4096]{1,0:T(8,128)(2,1)S(1)}, bf16[128,4096]{1,0:T(8,128)(2,1)}, u32[]{:S(2)}) copy-start(bf16[128,4096]{1,0:T(8,128)(2,1)} %param.12) | copy-start | bytes 3145732
  7.2 32.1 %all-gather.8.cloned.1.call-start = ((), (), s32[]{:S(2)}) async-start(), calls=%async_computation.5 | async-start | bytes 1310720 | tf_op jit(solution)/shard_map/all_gather | solution.py:67
  7.9 85.3 %all-gather.6.cloned.1.call-start = ((), (), s32[]{:S(2)}) async-start(), calls=%async_computation.4 | async-start | bytes 5242880 | tf_op jit(solution)/shard_map/all_gather | solution.py:66
  8.7 318.0 %all-reduce.7.cloned.1.call-start = ((), (), s32[]{:S(2)}) async-start(), calls=%async_computation.9 | async-start | bytes 2621440 | tf_op jit(solution)/shard_map/psum | solution.py:12
  11.3 85.6 %copy-start.11 = (s32[2]{0:T(128)}, s32[2]{0:T(128)S(1)}, u32[]{:S(2)}) copy-start(s32[2]{0:T(128)S(1)} %fusion.50) | copy-start | bytes 28
  95.5 333.3 %all-gather.4.cloned.1.call-start = ((), (), s32[]{:S(2)}) async-start(), calls=%async_computation.3 | async-start | bytes 17301504 | tf_op jit(solution)/shard_map/all_gather | solution.py:86
  96.1 528.5 %reduce-scatter.4.cloned.1.call-start = ((), (), s32[]{:S(2)}) async-start(), calls=%async_computation.6 | async-start | bytes 6291456 | tf_op jit(solution)/shard_map/reduce_scatter | solution.py:101
  97.2 6.6 copy-start.9
  100.2 3.6 copy-start.10
  337.2 99.8 %copy-start.5 = (bf16[1,64,1024]{2,1,0:T(8,128)(2,1)S(1)}, bf16[1,64,1024]{2,1,0:T(8,128)(2,1)}, u32[]{:S(2)}) copy-start(bf16[1,64,1024]{2,1,0:T(8,128)(2,1)} %get-tuple-element.42) | copy-start | bytes 393220
  337.2 99.8 %copy-start.6 = (bf16[1,64,1024]{2,1,0:T(8,128)(2,1)S(1)}, bf16[1,64,1024]{2,1,0:T(8,128)(2,1)}, u32[]{:S(2)}) copy-start(bf16[1,64,1024]{2,1,0:T(8,128)(2,1)} %get-tuple-element.43) | copy-start | bytes 393220
  337.2 100.6 %copy-start.7 = (f32[128,128,2]{1,0,2:T(8,128)S(1)}, f32[128,128,2]{1,0,2:T(8,128)}, u32[]{:S(2)}) copy-start(f32[128,128,2]{1,0,2:T(8,128)} %fusion.2) | copy-start | bytes 393220
  437.8 0.7 copy-start.3
  452.4 183.5 %reduce-scatter.8.cloned.1.call-start = ((), (), s32[]{:S(2)}) async-start(), calls=%async_computation.8 | async-start | bytes 1310720 | tf_op jit(solution)/shard_map/reduce_scatter | solution.py:125
  452.5 0.5 copy-start.14
  454.1 150.5 %copy-start.12 = (s32[2]{0:T(128)S(1)}, s32[2]{0:T(128)}, u32[]{:S(2)}) copy-start(s32[2]{0:T(128)} %copy-done.11) | copy-start | bytes 28
  454.1 150.5 %copy-start.13 = (pred[2]{0:T(512)(128)(4,1)S(1)}, pred[2]{0:T(512)(128)(4,1)}, u32[]{:S(2)}) copy-start(pred[2]{0:T(512)(128)(4,1)} %get-tuple-element.44) | copy-start | bytes 10
  604.6 3.3 copy-start.4
  607.8 82.0 %reduce-scatter.6.cloned.1.call-start = ((), (), s32[]{:S(2)}) async-start(), calls=%async_computation.7 | async-start | bytes 5242880 | tf_op jit(solution)/shard_map/reduce_scatter | solution.py:122
  614.0 1.4 copy-start.2
Sparse Core Ops, SparseCore 0:
  9.9 29.4 all-gather.7
  41.1 52.0 all-gather.5
  96.7 229.9 all-reduce.6
  328.5 100.2 all-gather.3
  452.6 83.4 reduce-scatter.3
  607.9 28.0 reduce-scatter.7
  639.3 50.4 reduce-scatter.5
where the time goes:
time: 697 us
  waiting for transfers between devices  452 us (65%)
  blocking collectives  156 us (22%)
  matrix products  44 us (6%)
  between operations  20.3 us (3%)
  local copies, waits for them, and re-layouts  15 us (2%)
  other arithmetic  8.8 us (1%)
    psum x1, waiting for transfers between devices, spread_2(): return lax.psum(block, axis)  223 us
    psum x1, blocking collectives, shards(): group_a, group_b = lax.psum((list_grad_a, list_grad_b), 'fsdp')  137 us
    all_gather x1, waiting for transfers between devices, shards(): whole_w = lax.all_gather(w_bc, 'fsdp', axis=0, tiled=True)  91.7 us
    reduce_scatter x1, waiting for transfers between devices, shards(): lax.psum_scatter(send_a.astype(jnp.bfloat16), 'tenant', scatter_dimension...  53.8 us
    all_gather x1, waiting for transfers between devices, shards(): lax.all_gather(a_store, 'tenant', axis=0, tiled=True)  52.2 us
    all_gather x1, waiting for transfers between devices, shards(): lax.all_gather(b_store, 'tenant', axis=0, tiled=True)  21.7 us
  transfers between devices with their start and end apart: 7, of which 6 were waited for; matrix products, arithmetic and copies ran while one was open for 6% of the time, Pallas kernels for 0%

commit v1 on v0

--- a/solution.py
+++ b/solution.py
@@ -9,7 +9,7 @@
 
 def spread_2(block, axis, holder):
     block = jnp.where(lax.axis_index(axis) == holder, block, jnp.zeros_like(block))
-    return lax.psum(block, axis)
+    return jnp.sum(lax.all_gather(block, axis), axis=0)
 
 
 def mix_state(proj_in, inner_x, step_size, decay_rate, block_len, heads_grp, state_dim):

time: 697 us -> 827 us (1.19)
  waiting for transfers between devices: 452 us -> 545 us
  other arithmetic: 8.8 us -> 34.5 us
    all_gather x0 -> x4, waiting for transfers between devices: none -> 312 us  [spread_2(): return jnp.sum(lax.all_gather(block, axis), axis=0)]
    psum x1 -> x0, waiting for transfers between devices: 223 us -> none  [spread_2(): return lax.psum(block, axis)]
    reduce_sum x0 -> x4, other arithmetic: none -> 23.7 us  [spread_2(): return jnp.sum(lax.all_gather(block, axis), axis=0)]
  transfers between devices with their start and end apart: 7 -> 10, of which waited for: 6 -> 9; matrix products, arithmetic and copies ran while one was open for 6% -> 8% of each run, Pallas kernels for 0% -> 0%
where the time goes in v1:
time: 827 us; the launch traced here: 826 us
  waiting for transfers between devices  545 us (66%)
  blocking collectives  159 us (19%)
  matrix products  48.7 us (6%)
  other arithmetic  34.5 us (4%)
  between operations  20.3 us (2%)
  local copies, waits for them, and re-layouts  18.1 us (2%)
    all_gather x4, waiting for transfers between devices, spread_2(): return jnp.sum(lax.all_gather(block, axis), axis=0)  312 us
    psum x1, blocking collectives, shards(): group_a, group_b = lax.psum((list_grad_a, list_grad_b), 'fsdp')  142 us
    all_gather x1, waiting for transfers between devices, shards(): whole_w = lax.all_gather(w_bc, 'fsdp', axis=0, tiled=True)  98 us
    reduce_scatter x1, waiting for transfers between devices, shards(): lax.psum_scatter(send_a.astype(jnp.bfloat16), 'tenant', scatter_dimension...  54.1 us
    all_gather x1, waiting for transfers between devices, shards(): lax.all_gather(a_store, 'tenant', axis=0, tiled=True)  51 us
    reduce_sum x4, other arithmetic, spread_2(): return jnp.sum(lax.all_gather(block, axis), axis=0)  23.7 us
    all_gather x1, waiting for transfers between devices, shards(): lax.all_gather(b_store, 'tenant', axis=0, tiled=True)  21.6 us
  transfers between devices with their start and end apart: 10, of which 9 were waited for; matrix products, arithmetic and copies ran while one was open for 8% of the time, Pallas kernels for 0%

profile of v1, /device:TPU:1, one launch (start us, length us, event | category | flops | bytes accessed | tf_op | source)
XLA Modules:
  0.0 826.0 jit_solution(8928028788950806523)
XLA Ops:
  17.7 21.6 %all-gather.16.cloned.1.call-done = bf16[8,64,1024]{2,1,0:T(8,128)(2,1)} async-done(((bf16[2,64,1024]{2,1,0:T(8,128)(2,1)}), bf16[8,64,1024]{2,1,0:T(8,128)(2,1)}) %all-gather.16.cloned.1.call-update) | async-done | bytes 1048592 | tf_op jit(solution)/shard_map/all_gather | solution.py:67
  39.3 1.7 dynamic-slice_select_fusion.2
  42.3 51.0 %all-gather.10.cloned.1.call-done = bf16[8,4096,64]{1,2,0:T(8,128)(2,1)} async-done(((bf16[2,4096,64]{1,2,0:T(8,128)(2,1)}), bf16[8,4096,64]{1,2,0:T(8,128)(2,1)}) %all-gather.10.cloned.1.call-update) | async-done | bytes 4194320 | tf_op jit(solution)/shard_map/all_gather | solution.py:66
  93.3 2.3 dynamic-slice_select_fusion
  98.7 1.6 copy.54
  100.4 3.6 fusion.2
  104.0 59.2 %all-gather.18.cloned.1.call-done = bf16[32,64,1024]{2,1,0:T(8,128)(2,1)} async-done(((bf16[1,64,1024]{2,1,0:T(8,128)(2,1)}), bf16[32,64,1024]{2,1,0:T(8,128)(2,1)}) %all-gather.18.cloned.1.call-update) | async-done | bytes 4194320 | tf_op jit(solution)/shard_map/all_gather | solution.py:12
  163.3 3.1 reduce_sum.63
  166.4 65.6 %all-gather.20.cloned.1.call-done = bf16[32,64,1024]{2,1,0:T(8,128)(2,1)} async-done(((bf16[1,64,1024]{2,1,0:T(8,128)(2,1)}), bf16[32,64,1024]{2,1,0:T(8,128)(2,1)}) %all-gather.20.cloned.1.call-update) | async-done | bytes 4194320 | tf_op jit(solution)/shard_map/all_gather | solution.py:12
  232.1 3.1 reduce_sum.64
  235.2 98.0 %all-gather.8.cloned.1.call-done = bf16[8192,1024]{1,0:T(8,128)(2,1)} async-done(((bf16[256,1024]{1,0:T(8,128)(2,1)}), bf16[8192,1024]{1,0:T(8,128)(2,1)}) %all-gather.8.cloned.1.call-update) | async-done | bytes 16777232 | tf_op jit(solution)/shard_map/all_gather | solution.py:86
  333.2 8.9 %fusion.63 = f32[128,1024]{1,0:T(8,128)} fusion(bf16[128,8192]{1,0:T(8,128)(2,1)S(1)} %copy-done, bf16[8192,1024]{1,0:T(8,128)(2,1)} %all-gather.8.cloned.1.call-done), kind=kOutput, calls=%fused_computation.97 | convolution fusion | flops 2147483648 | bytes 19398656 | tf_op jit(solution)/shard_map/dot_general | solution.py:87
  342.1 93.0 %all-gather.12.cloned.1.call-done = bf16[32,4096,64]{1,2,0:T(8,128)(2,1)} async-done(((bf16[1,4096,64]{1,2,0:T(8,128)(2,1)}), bf16[32,4096,64]{1,2,0:T(8,128)(2,1)}) %all-gather.12.cloned.1.call-update) | async-done | bytes 16777232 | tf_op jit(solution)/shard_map/all_gather | solution.py:12
  435.1 8.7 %reduce_sum.61 = bf16[4096,64]{0,1:T(8,128)(2,1)S(1)} reduce(bf16[32,4096,64]{1,2,0:T(8,128)(2,1)} %all-gather.12.cloned.1.call-done, bf16[]{:T(256)} %constant.85.clone.1), dimensions={0}, to_apply=%region_1.2 | reduce | flops 8126464 | bytes 17301506 | tf_op jit(solution)/shard_map/reduce_sum | solution.py:12
  443.8 93.9 %all-gather.14.cloned.1.call-done = bf16[32,4096,64]{1,2,0:T(8,128)(2,1)} async-done(((bf16[1,4096,64]{1,2,0:T(8,128)(2,1)}), bf16[32,4096,64]{1,2,0:T(8,128)(2,1)}) %all-gather.14.cloned.1.call-update) | async-done | bytes 16777232 | tf_op jit(solution)/shard_map/all_gather | solution.py:12
  537.7 8.7 %reduce_sum.62 = bf16[4096,64]{0,1:T(8,128)(2,1)S(1)} reduce(bf16[32,4096,64]{1,2,0:T(8,128)(2,1)} %all-gather.14.cloned.1.call-done, bf16[]{:T(256)} %constant.85.clone.1), dimensions={0}, to_apply=%region_2.3 | reduce | flops 8126464 | bytes 17301506 | tf_op jit(solution)/shard_map/reduce_sum | solution.py:12
  546.9 9.5 %psum.28 = bf16[1,128,64]{1,2,0:T(8,128)(2,1)S(1)} all-reduce(f32[1,128,64]{1,2,0:T(8,128)S(1)} %convolution_bitcast_fusion.3), channel_id=1, replica_groups=mesh['fsdp'=32,'tenant'=4,'tensor'=2] {'tensor'}, use_global_device_ids=true, to_apply=%region_3.4 | all-reduce | flops 8192 | bytes 49152 | tf_op jit(solution)/shard_map/psum | solution.py:85
  557.1 2.0 fusion.18
  560.6 1.4 convolution_bitcast_fusion
  565.0 13.5 %fusion.64 = f32[128,8192]{1,0:T(8,128)} fusion(bf16[128,1024]{0,1:T(8,128)(2,1)S(1)} %bitcast.113, bf16[8192,1024]{1,0:T(8,128)(2,1)} %all-gather.8.cloned.1.call-done), kind=kOutput, calls=%fused_computation.98 | convolution fusion | flops 2147483648 | bytes 21233664 | tf_op jit(solution)/shard_map/dot_general | solution.py:100
  579.1 1.7 convolution_bitcast_fusion.4
  580.8 7.7 psum.29
  588.8 3.2 broadcast_multiply_fusion
  594.0 141.7 %all-reduce.4 = (bf16[2,4096,64]{1,0,2:T(2,128)(2,1)}, bf16[2,1024,64]{1,0,2:T(2,128)(2,1)S(1)}) all-reduce(f32[2,4096,64]{1,0,2:T(2,128)} %broadcast_multiply_fusion, f32[2,1024,64]{1,0,2:T(2,128)} %broadcast_multiply_fusion.1), channel_id=1, replica_groups=mesh['fsdp'=32,'tenant'=4,'tensor'=2] {'fsdp'}, use_global_device_ids=true, to_apply=%region_9.10 | all-reduce | flops 655360 | bytes 3932160 | tf_op jit(solution)/shard_map/psum | solution.py:111
  736.3 1.6 copy.58
  738.2 2.9 convolution_convert_fusion
  741.1 4.3 copy.57
  747.5 7.1 fusion.15
  754.6 2.3 copy.59
  756.9 3.0 fusion
  759.9 5.1 reduce-scatter.8.cloned.1.call-done
  765.1 54.1 %reduce-scatter.6.cloned.1.call-done = bf16[2,4096,64]{1,2,0:T(8,128)(2,1)} async-done(((bf16[8,4096,64]{1,2,0:T(8,128)(2,1)}), bf16[2,4096,64]{1,2,0:T(8,128)(2,1)}) %reduce-scatter.6.cloned.1.call-update) | async-done | bytes 1048592 | tf_op jit(solution)/shard_map/reduce_scatter | solution.py:122
  (77 shorter events, 20.5 us)
Async XLA Ops:
  7.2 326.0 %copy-start = (bf16[128,8192]{1,0:T(8,128)(2,1)S(1)}, bf16[128,8192]{1,0:T(8,128)(2,1)}, u32[]{:S(2)}) copy-start(bf16[128,8192]{1,0:T(8,128)(2,1)} %param.11) | copy-start | bytes 6291460
  7.2 89.8 %copy-start.7 = (f32[128,64]{0,1:T(8,128)S(1)}, f32[128,64]{0,1:T(8,128)}, u32[]{:S(2)}) copy-start(f32[128,64]{0,1:T(8,128)} %param.13) | copy-start | bytes 98308
  7.2 89.9 %copy-start.14 = (f32[64]{0:T(128)S(1)}, f32[64]{0:T(128)}, u32[]{:S(2)}) copy-start(f32[64]{0:T(128)} %param.14) | copy-start | bytes 772
  7.2 90.2 %copy-start.2 = (bf16[128,4096]{1,0:T(8,128)(2,1)S(1)}, bf16[128,4096]{1,0:T(8,128)(2,1)}, u32[]{:S(2)}) copy-start(bf16[128,4096]{1,0:T(8,128)(2,1)} %param.12) | copy-start | bytes 3145732
  7.2 32.1 %all-gather.16.cloned.1.call-start = ((), (), s32[]{:S(2)}) async-start(), calls=%async_computation.7 | async-start | bytes 1310720 | tf_op jit(solution)/shard_map/all_gather | solution.py:67
  7.9 85.3 %all-gather.10.cloned.1.call-start = ((), (), s32[]{:S(2)}) async-start(), calls=%async_computation.4 | async-start | bytes 5242880 | tf_op jit(solution)/shard_map/all_gather | solution.py:66
  8.7 154.6 %all-gather.18.cloned.1.call-start = ((), (), s32[]{:S(2)}) async-start(), calls=%async_computation.8 | async-start | bytes 4325376 | tf_op jit(solution)/shard_map/all_gather | solution.py:12
  11.4 85.8 %copy-start.10 = (s32[2]{0:T(128)}, s32[2]{0:T(128)S(1)}, u32[]{:S(2)}) copy-start(s32[2]{0:T(128)S(1)} %fusion.50) | copy-start | bytes 28
  41.0 191.0 %all-gather.20.cloned.1.call-start = ((), (), s32[]{:S(2)}) async-start(), calls=%async_computation.9 | async-start | bytes 4325376 | tf_op jit(solution)/shard_map/all_gather | solution.py:12
  41.6 291.6 %all-gather.8.cloned.1.call-start = ((), (), s32[]{:S(2)}) async-start(), calls=%async_computation.3 | async-start | bytes 17301504 | tf_op jit(solution)/shard_map/all_gather | solution.py:86
  42.2 392.9 %all-gather.12.cloned.1.call-start = ((), (), s32[]{:S(2)}) async-start(), calls=%async_computation.5 | async-start | bytes 17301504 | tf_op jit(solution)/shard_map/all_gather | solution.py:12
  95.5 442.2 %all-gather.14.cloned.1.call-start = ((), (), s32[]{:S(2)}) async-start(), calls=%async_computation.6 | async-start | bytes 17301504 | tf_op jit(solution)/shard_map/all_gather | solution.py:12
  96.3 660.6 %reduce-scatter.4.cloned.1.call-start = ((), (), s32[]{:S(2)}) async-start(), calls=%async_computation.10 | async-start | bytes 6291456 | tf_op jit(solution)/shard_map/reduce_scatter | solution.py:101
  97.4 6.6 copy-start.8
  100.4 3.6 copy-start.9
  235.2 321.3 %copy-start.1 = (bf16[64,1024]{1,0:T(8,128)(2,1)}, bf16[64,1024]{1,0:T(8,128)(2,1)S(1)}, u32[]{:S(2)}) copy-start(bf16[64,1024]{1,0:T(8,128)(2,1)S(1)} %reduce_sum.64) | copy-start | bytes 393220
  556.5 0.6 copy-start.6
  560.6 2.6 copy-start.3
  560.6 2.6 copy-start.5
  578.5 186.5 %reduce-scatter.8.cloned.1.call-start = ((), (), s32[]{:S(2)}) async-start(), calls=%async_computation.12 | async-start | bytes 1310720 | tf_op jit(solution)/shard_map/reduce_scatter | solution.py:125
  580.8 12.1 %copy-start.13 = (f32[2]{0:T(128)S(1)}, f32[2]{0:T(128)}, u32[]{:S(2)}) copy-start(f32[2]{0:T(128)} %compare_convert_fusion) | copy-start | bytes 28
  588.5 147.2 %copy-start.11 = (s32[2]{0:T(128)S(1)}, s32[2]{0:T(128)}, u32[]{:S(2)}) copy-start(s32[2]{0:T(128)} %copy-done.10) | copy-start | bytes 28
  588.5 147.2 %copy-start.12 = (pred[2]{0:T(512)(128)(4,1)S(1)}, pred[2]{0:T(512)(128)(4,1)}, u32[]{:S(2)}) copy-start(pred[2]{0:T(512)(128)(4,1)} %get-tuple-element.40) | copy-start | bytes 10
  737.9 81.3 %reduce-scatter.6.cloned.1.call-start = ((), (), s32[]{:S(2)}) async-start(), calls=%async_computation.11 | async-start | bytes 5242880 | tf_op jit(solution)/shard_map/reduce_scatter | solution.py:122
  745.4 0.9 copy-start.4
Sparse Core Ops, SparseCore 0:
  9.9 29.4 all-gather.15
  41.1 52.0 all-gather.9
  95.7 67.5 all-gather.17
  165.6 66.4 all-gather.19
  233.8 99.3 all-gather.7
  334.9 100.1 all-gather.11
  437.5 100.1 all-gather.13
  578.6 79.7 reduce-scatter.3
  738.0 27.0 reduce-scatter.7
  768.0 51.0 reduce-scatter.5
